TPU v7x, 32 devices: a whole 2x2x4 slice. The times are simulated.
32 devices in a mesh: groups: 2 (over y), row: 4 (over z), col: 4 (over x, core).
Axes of the slice: x: 2, y: 2, z: 4, core: 2. Of those that a mesh axis runs over, the one named last changes fastest.
Arguments:
- hidden: bfloat16 [2048, 8192], P(('groups', 'row'), 'col'), parts along dimension 0, may hold values from -6 to 6
- w_gate_z: bfloat16 [8192, 16384], P('col', 'row'), may hold values from -0.0625 to 0.0625
- w_input_x: bfloat16 [8192, 16384], P('col', 'row'), may hold values from -0.0625 to 0.0625
- w_input_bc: bfloat16 [8192, 4096], P('col', 'row'), may hold values from -0.0625 to 0.0625
- w_input_dt: bfloat16 [8192, 256], P('col', 'row'), may hold values from -0.0625 to 0.0625
- conv_kernel_x: bfloat16 [4, 16384], P(None, 'row'), may hold values from -3 to 3
- conv_kernel_bc: bfloat16 [4, 4096], P(None, 'row'), may hold values from -3 to 3
- conv_state_x: bfloat16 [6, 16384], P('groups', 'row'), parts along dimension 0, may hold values from -6 to 6
- conv_state_bc: bfloat16 [6, 4096], P('groups', 'row'), parts along dimension 0, may hold values from -6 to 6
- dt_bias: float32 [256], P('row'), may hold values from -5 to -3
- a_log: float32 [256], P('row'), may hold values from -3 to 1.1
- d_skip: float32 [256], P('row'), may hold values from 0.5 to 1.5
- norm_gain: float32 [16384], P('row'), may hold values from 0.1 to 1.9
- ssm_state: float32 [512, 64, 256], P(('groups', 'row')), parts along dimension 0, may hold values from -6 to 6
- w_output: bfloat16 [16384, 8192], P('row', 'col'), may hold values from -0.046875 to 0.046875
Outputs:
- mixed: bfloat16 [2048, 8192], P(('groups', 'row'), 'col'), parts along dimension 0
There are 2 independent parts, one for each index of `groups`. A program takes and returns all parts, laid end to end along the dimension named above; an argument that names none is the same for every part. Nothing has to cross between parts.
All inputs are finite; a program needn't handle non-finite values.
Results may differ from a plain program's by a relative error of at most 0.02.
Values may be sent and summed in bfloat16 or wider, within the bound.
A program may use at most 256 MiB of HBM per device.

v0:
```python
import jax
import jax.numpy as jnp
from jax import lax
from jax.sharding import PartitionSpec as P

highest = lax.Precision.HIGHEST


def from_behind(value, axis, steps):
    count = lax.axis_size(axis)
    first, last = (max(0, -steps), min(count, count - steps))
    return lax.ppermute(value, axis, [(source, source + steps) for source in range(first, last)])


def entering(value, axis, combine, identity):
    count, mine = (lax.axis_size(axis), lax.axis_index(axis))
    everything = jax.tree.map(
        lambda part, kind: lax.all_gather(part.astype(kind), axis),
        value,
        (jnp.bfloat16, jnp.bfloat16),
    )
    start = jax.tree.map(
        lambda part, zero: jnp.broadcast_to(jnp.asarray(zero, part.dtype), part.shape),
        value,
        identity,
    )

    def turn(k, before):
        reached = k < mine
        new = combine(
            before, jax.tree.map(lambda part, own: part[k].astype(own.dtype), everything, value)
        )
        return jax.tree.map(lambda a, b: jnp.where(reached, a, b), new, before)

    return lax.fori_loop(0, count, turn, start)


def swapped(value, axis, bit):
    mask = 2**bit
    pairs = [(source, source ^ mask) for source in range(lax.axis_size(axis))]
    return lax.ppermute(value, axis, pairs)


def convolve_silu(previous, current, kernel):
    stacked = jnp.concatenate([previous, current], axis=0).astype(jnp.float32)
    length = current.shape[0]
    accum = jnp.zeros(current.shape, jnp.float32)
    for offset in range(kernel.shape[0]):
        accum = (
            accum + kernel[offset].astype(jnp.float32)[None, :] * stacked[offset : offset + length]
        )
    return jax.nn.silu(accum).astype(jnp.bfloat16)


def block_parts(x_block, b_block, c_block, dt_block, log_block):
    length = x_block.shape[0]
    cumulative = jnp.cumsum(log_block, axis=0)
    scores = jnp.einsum("tjn,sjn->jts", c_block, b_block, precision=highest)
    spans = cumulative.T[:, :, None] - cumulative.T[:, None, :]
    causal = (jnp.arange(length)[:, None] >= jnp.arange(length)[None, :])[None, :, :]
    decay_mask = jnp.where(causal, jnp.exp(jnp.where(causal, spans, 0.0)), 0.0)
    mixing = scores * decay_mask * dt_block.T[:, None, :]
    intra = jnp.einsum("jts,sjp->tjp", mixing, x_block, precision=highest)
    tail_weight = jnp.exp(cumulative[-1][None, :] - cumulative) * dt_block
    local_state = jnp.einsum("sj,sjp,sjn->jpn", tail_weight, x_block, b_block, precision=highest)
    return (intra, cumulative, local_state)


def local_scan(x_heads, b_heads, c_heads, steps_dt, log_decay):
    length, heads_here, head_size = x_heads.shape
    state_size = b_heads.shape[2]
    block_len = min(length, 256)
    blocks = length // block_len

    def to_blocks(array):
        return array.reshape((blocks, block_len) + array.shape[1:])

    def advance(carry_state, inputs):
        x_block, b_block, c_block, dt_block, log_block = inputs
        intra, cumulative, local_state = block_parts(x_block, b_block, c_block, dt_block, log_block)
        carried = jnp.exp(cumulative)[:, :, None] * jnp.einsum(
            "tjn,jpn->tjp", c_block, carry_state, precision=highest
        )
        new_state = jnp.exp(cumulative[-1])[:, None, None] * carry_state + local_state
        return (new_state, intra + carried)

    initial = jnp.zeros((heads_here, head_size, state_size), jnp.float32)
    final_state, outputs = lax.scan(
        advance,
        initial,
        (
            to_blocks(x_heads),
            to_blocks(b_heads),
            to_blocks(c_heads),
            to_blocks(steps_dt),
            to_blocks(log_decay),
        ),
    )
    return (outputs.reshape(length, heads_here, head_size), final_state)


def chain_combine(earlier, later_part):
    return (earlier[0] * later_part[0], later_part[0][:, None, None] * earlier[1] + later_part[1])


def local(
    hidden,
    w_gate_z,
    w_input_x,
    w_input_bc,
    w_input_dt,
    conv_kernel_x,
    conv_kernel_bc,
    conv_state_x,
    conv_state_bc,
    dt_bias,
    a_log,
    d_skip,
    norm_gain,
    ssm_state,
    w_output,
):
    channels = w_gate_z.shape[1]
    bc_local = w_input_bc.shape[1]
    heads_local = w_input_dt.shape[1]
    head_size = ssm_state.shape[1]
    state_size = ssm_state.shape[2]
    kernel_len = conv_kernel_x.shape[0]
    weights = jnp.concatenate([w_gate_z, w_input_x, w_input_bc, w_input_dt], axis=1)
    partial_proj = jnp.dot(
        lax.all_gather(hidden, "row", axis=0, tiled=True),
        weights,
        preferred_element_type=jnp.float32,
    )
    summed = lax.psum_scatter(
        partial_proj.astype(jnp.bfloat16), "col", scatter_dimension=0, tiled=True
    ).astype(jnp.float32)
    gate_z = summed[:, :channels].astype(jnp.bfloat16)
    input_x = summed[:, channels : 2 * channels].astype(jnp.bfloat16)
    input_bc = summed[:, 2 * channels : 2 * channels + bc_local].astype(jnp.bfloat16)
    dt_raw = summed[:, 2 * channels + bc_local :]
    tail_rows = jnp.concatenate(
        [input_x[-(kernel_len - 1) :], input_bc[-(kernel_len - 1) :]], axis=1
    )
    arrived = from_behind(tail_rows, "col", 1)
    first_col = lax.axis_index("col") == 0
    prev_x = jnp.where(first_col, conv_state_x, arrived[:, :channels])
    prev_bc = jnp.where(first_col, conv_state_bc, arrived[:, channels:])
    conv_x = convolve_silu(prev_x, input_x, conv_kernel_x)
    conv_bc = convolve_silu(prev_bc, input_bc, conv_kernel_bc)
    tokens_here = conv_x.shape[0]
    gathered_bc = lax.all_gather(conv_bc, "row", axis=1, tiled=True)
    bc_total = gathered_bc.shape[1]
    group_count = bc_total // (2 * state_size)
    heads_total = heads_local * lax.axis_size("row")
    per_group = heads_total // group_count
    head_ids = lax.axis_index("row") * heads_local + jnp.arange(heads_local, dtype=jnp.int32)
    group_ids = head_ids // per_group
    onehot = group_ids[:, None] == jnp.arange(group_count, dtype=jnp.int32)[None, :]
    b_groups = gathered_bc[:, : bc_total // 2].reshape(tokens_here, group_count, state_size)
    c_groups = gathered_bc[:, bc_total // 2 :].reshape(tokens_here, group_count, state_size)
    b_heads = jnp.einsum(
        "tgn,jg->tjn", b_groups, onehot.astype(jnp.bfloat16), preferred_element_type=jnp.float32
    )
    c_heads = jnp.einsum(
        "tgn,jg->tjn", c_groups, onehot.astype(jnp.bfloat16), preferred_element_type=jnp.float32
    )
    steps_dt = jax.nn.softplus(dt_raw + dt_bias[None, :])
    log_decay = steps_dt * (-jnp.exp(a_log))[None, :]
    x_heads = conv_x.astype(jnp.float32).reshape(tokens_here, heads_local, head_size)
    local_out, local_state = local_scan(x_heads, b_heads, c_heads, steps_dt, log_decay)
    cumulative = jnp.cumsum(log_decay, axis=0)
    decay_total = jnp.exp(cumulative[-1])
    prefix_decay, prefix_state = entering(
        (decay_total, local_state),
        "col",
        chain_combine,
        (jnp.ones_like(decay_total), jnp.zeros_like(local_state)),
    )
    incoming = prefix_state + prefix_decay[:, None, None] * ssm_state
    carried = jnp.exp(cumulative)[:, :, None] * jnp.einsum(
        "tjn,jpn->tjp", c_heads, incoming, precision=highest
    )
    y_heads = local_out + carried + d_skip[None, :, None] * x_heads
    gated = y_heads * jax.nn.silu(gate_z.astype(jnp.float32)).reshape(
        tokens_here, heads_local, head_size
    )
    head_squares = jnp.sum(gated * gated, axis=2)
    if per_group <= heads_local:
        group_sums = jnp.sum(
            head_squares.reshape(tokens_here, heads_local // per_group, per_group), axis=2
        )
        head_mean = jnp.repeat(group_sums, per_group, axis=1) / (per_group * head_size)
    else:
        partial_squares = jnp.sum(head_squares, axis=1, keepdims=True)
        for bit_number in range((per_group // heads_local).bit_length() - 1):
            partial_squares = partial_squares + swapped(partial_squares, "row", bit_number)
        head_mean = jnp.broadcast_to(partial_squares, (tokens_here, heads_local)) / (
            per_group * head_size
        )
    normed = gated * lax.rsqrt(head_mean + 1e-05)[:, :, None]
    y_normed = (normed.reshape(tokens_here, channels) * norm_gain[None, :]).astype(jnp.bfloat16)
    all_tokens = lax.all_gather(y_normed, "col", axis=0, tiled=True)
    return lax.psum_scatter(
        jnp.dot(all_tokens, w_output, preferred_element_type=jnp.float32).astype(jnp.bfloat16),
        "row",
        scatter_dimension=0,
        tiled=True,
    )


def solution(mesh):
    return jax.shard_map(
        local,
        mesh=mesh,
        in_specs=(
            P(("groups", "row"), "col"),
            P("col", "row"),
            P("col", "row"),
            P("col", "row"),
            P("col", "row"),
            P(None, "row"),
            P(None, "row"),
            P("groups", "row"),
            P("groups", "row"),
            P("row"),
            P("row"),
            P("row"),
            P("row"),
            P(("groups", "row"), None, None),
            P("row", "col"),
        ),
        out_specs=P(("groups", "row"), "col"),
        check_vma=False,
    )
```

profile of v0, /device:TPU:0, one launch (start us, length us, event | category | flops | bytes accessed | tf_op | source)
XLA Modules:
  0.0 785.3 jit_solution(13589428115134903799)
XLA Ops:
  8.5 83.9 %all-gather.7.cloned.1.call-done = bf16[1024,2048]{1,0:T(8,128)(2,1)} async-done(((bf16[256,2048]{1,0:T(8,128)(2,1)}), bf16[1024,2048]{1,0:T(8,128)(2,1)}) %all-gather.7.cloned.1.call-update) | async-done | bytes 4194320 | tf_op jit(solution)/shard_map/all_gather | solution.py:131
  92.4 74.9 %convert_bitcast_fusion = bf16[1024,9280]{0,1:T(8,128)(2,1)} fusion(bf16[1024,2048]{1,0:T(8,128)(2,1)} %all-gather.7.cloned.1.call-done, bf16[2048,64]{1,0:T(8,128)(2,1)S(1)} %copy.59, bf16[2048,1024]{1,0:T(8,128)(2,1)} %param.20, bf16[2048,4096]{1,0:T(8,128)(2,1)} %param.19, bf16[2048,4096]{1,0:T(8,128)(2,1)} %param.18), kind=kOutput, calls=%fused_computation.13 | convolution fusion | flops 39084687360 | bytes 61210624 | tf_op jit(solution)/shard_map/dot_general | solution.py:130
  168.2 138.1 %reduce-scatter.3.cloned.1.call-done = bf16[256,9280]{0,1:T(8,128)(2,1)} async-done(((bf16[1024,9280]{0,1:T(8,128)(2,1)}), bf16[256,9280]{0,1:T(8,128)(2,1)}) %reduce-scatter.3.cloned.1.call-update) | async-done | bytes 4751376 | tf_op jit(solution)/shard_map/reduce_scatter | solution.py:135
  312.7 2.3 multiply_convert_fusion.1
  318.9 6.3 multiply_convert_fusion
  325.2 37.6 %all-gather.9.cloned.1.call-done = bf16[256,4096]{0,1:T(8,128)(2,1)} async-done(((bf16[256,1024]{0,1:T(8,128)(2,1)}), bf16[256,4096]{0,1:T(8,128)(2,1)}) %all-gather.9.cloned.1.call-update) | async-done | bytes 2097168 | tf_op jit(solution)/shard_map/all_gather | solution.py:152
  362.8 3.0 fusion.66
  367.7 8.1 %convolution_bitcast_fusion = f32[256,64,256]{2,1,0:T(8,128)} fusion(bf16[256,8,256]{2,1,0:T(8,128)(2,1)S(1)} %copy.64, s32[64]{0:T(128)S(1)} %and_select_fusion), kind=kOutput, calls=%fused_computation.30 | convolution fusion | flops 67109376 | bytes 17826048 | tf_op jit(solution)/shard_map/tgn,jg->tjn/dot_general | solution.py:162
  375.8 26.4 %add_convert_fusion = bf16[64,64,256]{2,1,0:T(8,128)(2,1)} fusion(f32[64]{0:T(128)S(1)} %exponential_multiply_fusion.1, f32[256,64,256]{2,1,0:T(8,128)} %convolution_bitcast_fusion, bf16[256,64,64]{0,2,1:T(8,128)(2,1)S(1)} %bitcast.89, f32[256,64]{0,1:T(8,128)S(1)} %get-tuple-element.177), kind=kOutput, calls=%fused_computation.62 | convolution fusion | flops 3225419776 | bytes 21037312 | tf_op jit(solution)/shard_map/while/body/eval_jaxpr/sj,sjp,sjn->jpn/dot_general | solution.py:65
  402.5 5.0 all-gather.1
  407.6 5.4 convert_multiply_fusion
  415.0 8.1 %convolution_bitcast_fusion.1 = f32[256,64,256]{2,1,0:T(8,128)} fusion(bf16[256,8,256]{2,1,0:T(8,128)(2,1)S(1)} %copy.63, s32[64]{0:T(128)S(1)} %and_select_fusion), kind=kOutput, calls=%fused_computation.31 | convolution fusion | flops 67109376 | bytes 17826048 | tf_op jit(solution)/shard_map/tgn,jg->tjn/dot_general | solution.py:165
  423.1 86.9 %fusion.20 = f32[64,256,256]{2,1,0:T(8,128)} fusion(f32[256,64,256]{2,1,0:T(8,128)} %convolution_bitcast_fusion, f32[256,64,256]{2,1,0:T(8,128)} %convolution_bitcast_fusion.1), kind=kOutput, calls=%fused_computation.23 | convolution fusion | flops 12884901888 | bytes 50331648 | tf_op jit(solution)/shard_map/while/body/eval_jaxpr/tjn,sjn->jts/dot_general | solution.py:58
  510.1 17.3 %fusion.11 = f32[64,64,256]{2,1,0:T(8,128)} fusion(bf16[256,64,64]{0,2,1:T(8,128)(2,1)S(1)} %bitcast.90, f32[64,256,256]{2,1,0:T(8,128)} %fusion.20, f32[64,256]{1,0:T(8,128)S(1)} %copy-done.1, f32[64,256]{1,0:T(8,128)S(1)} %get-tuple-element.181, pred[256,256]{1,0:T(8,128)(4,1)S(1)} %iota_compare_fusion), kind=kOutput, calls=%fused_computation.14 | convolution fusion | flops 3242196992 | bytes 23265280 | tf_op jit(solution)/shard_map/while/body/eval_jaxpr/jts,sjp->tjp/dot_general | solution.py:63
  527.4 22.5 %while.10 = (s32[]{:T(128)}, f32[64]{0:T(128)S(1)}, f32[64,64,256]{2,1,0:T(8,128)}, s32[]{:T(128)}, bf16[4,64]{1,0:T(4,128)(2,1)S(1)}, /*index=5*/bf16[4,64,64,256]{3,2,1,0:T(8,128)(2,1)}, s32[]{:T(128)}, s32[]{:T(128)}) while((s32[]{:T(128)}, f32[64]{0:T(128)S(1)}, f32[64,64,256]{2,1,0:T(8,128)}, s32[]{:T(128)}, ...), condition=%wide.region_4.5_spmd.clone, body=%wide.region_3.4_spmd.clone.sunk | while | flops 5243140 | bytes 10487035 | solution.py:35
  527.4 4.7 fusion.77
  532.1 5.9 fusion.77
  538.0 5.9 fusion.77
  544.0 5.9 fusion.77
  549.9 34.2 %fusion.22 = f32[64,64,256]{2,1,0:T(8,128)} fusion(f32[256,64,256]{2,1,0:T(8,128)} %convolution_bitcast_fusion.1, f32[64,64,256]{2,1,0:T(8,128)} %get-tuple-element.139, f32[64,64,256]{2,1,0:T(8,128)} %param.30, f32[64]{0:T(128)S(1)} %get-tuple-element.140), kind=kOutput, calls=%fused_computation.25 | convolution fusion | flops 3223322624 | bytes 29360384 | tf_op jit(solution)/shard_map/tjn,jpn->tjp/dot_general | solution.py:181
  584.1 32.7 %multiply_reduce_fusion = (f32[256,64]{0,1:T(8,128)S(1)}, f32[256,64,64]{0,2,1:T(8,128)S(1)}) fusion(f32[256,64,64]{0,2,1:T(8,128)} %bitcast.92, bf16[256,64,64]{0,2,1:T(8,128)(2,1)S(1)} %bitcast.91, f32[64]{0:T(128)S(1)} %copy-done.7, f32[64,64,256]{2,1,0:T(8,128)} %fusion.22, f32[256,64,256]{2,1,0:T(8,128)} %convolution_bitcast_fusion.1, ...), kind=kOutput, calls=%fused_computation.59 | convolution fusion | flops 3231694848 | bytes 35782912 | tf_op jit(solution)/shard_map/while/body/eval_jaxpr/tjn,jpn->tjp/dot_general | solution.py:81
  619.6 57.6 %all-gather.11.cloned.1.call-done = bf16[1024,4096]{0,1:T(8,128)(2,1)} async-done(((bf16[256,4096]{0,1:T(8,128)(2,1)}), bf16[1024,4096]{0,1:T(8,128)(2,1)}) %all-gather.11.cloned.1.call-update) | async-done | bytes 8388624 | tf_op jit(solution)/shard_map/all_gather | solution.py:203
  677.2 23.9 %convolution_convert_fusion = bf16[1024,2048]{1,0:T(8,128)(2,1)} fusion(bf16[1024,4096]{0,1:T(8,128)(2,1)} %all-gather.11.cloned.1.call-done, bf16[4096,2048]{1,0:T(8,128)(2,1)} %param.31), kind=kOutput, calls=%fused_computation.64 | convolution fusion | flops 17181966336 | bytes 29360128 | tf_op jit(solution)/shard_map/dot_general | solution.py:205
  701.1 76.9 %reduce-scatter.5.cloned.1.call-done = bf16[256,2048]{1,0:T(8,128)(2,1)} async-done(((bf16[1024,2048]{1,0:T(8,128)(2,1)}), bf16[256,2048]{1,0:T(8,128)(2,1)}) %reduce-scatter.5.cloned.1.call-update) | async-done | bytes 1048592 | tf_op jit(solution)/shard_map/reduce_scatter | solution.py:204
  (75 shorter events, 19.9 us)
Async XLA Ops:
  6.5 85.9 %all-gather.7.cloned.1.call-start = ((), (), s32[]{:S(2)}) async-start(), calls=%async_computation.2 | async-start | bytes 5242880 | tf_op jit(solution)/shard_map/all_gather | solution.py:131
  7.3 299.0 %reduce-scatter.3.cloned.1.call-start = ((), (), s32[]{:S(2)}) async-start(), calls=%async_computation.3 | async-start | bytes 23756800 | tf_op jit(solution)/shard_map/reduce_scatter | solution.py:135
  167.3 0.7 copy-start.8
  167.3 0.7 copy-start.3
  167.3 0.8 copy-start
  167.3 142.9 %copy-start.6 = (f32[64]{0:T(128)S(1)}, f32[64]{0:T(128)}, u32[]{:S(2)}) copy-start(f32[64]{0:T(128)} %param.26) | copy-start | bytes 772
  167.4 195.5 %all-gather.9.cloned.1.call-start = ((), (), s32[]{:S(2)}) async-start(), calls=%async_computation.4 | async-start | bytes 2621440 | tf_op jit(solution)/shard_map/all_gather | solution.py:152
  308.0 4.0 copy-start.5
  308.0 4.3 slice-start.1
  308.5 3.5 collective-permute-start
  312.1 4.9 copy-start.2
  312.3 5.2 slice-start
  315.0 212.4 %all-gather.13.cloned.1.call-start = ((), (), s32[]{:S(2)}) async-start(), calls=%async_computation.7 | async-start | bytes 10485760 | tf_op jit(solution)/shard_map/all_gather | solution.py:18
  402.2 275.0 %all-gather.11.cloned.1.call-start = ((), (), s32[]{:S(2)}) async-start(), calls=%async_computation.5 | async-start | bytes 10485760 | tf_op jit(solution)/shard_map/all_gather | solution.py:203
  423.1 87.0 %copy-start.1 = (f32[64,256]{1,0:T(8,128)S(1)}, f32[64,256]{1,0:T(8,128)}, u32[]{:S(2)}) copy-start(f32[64,256]{1,0:T(8,128)} %get-tuple-element.176) | copy-start | bytes 196612
  549.9 34.2 %copy-start.7 = (f32[64]{0:T(128)S(1)}, f32[64]{0:T(128)}, u32[]{:S(2)}) copy-start(f32[64]{0:T(128)} %param.28) | copy-start | bytes 772
  616.8 0.7 copy-start.4
  619.6 158.4 %reduce-scatter.5.cloned.1.call-start = ((), (), s32[]{:S(2)}) async-start(), calls=%async_computation.6 | async-start | bytes 5242880 | tf_op jit(solution)/shard_map/reduce_scatter | solution.py:204
Sparse Core Ops, SparseCore 0:
  8.9 83.4 all-gather.6
  167.5 138.7 reduce-scatter.2
  315.1 47.6 all-gather.8
  402.4 56.9 all-gather.12
  619.7 57.4 all-gather.10
  701.2 76.7 reduce-scatter.4
where the time goes:
time: 793 us; the launch traced here: 785 us
  waiting for transfers between devices  395 us (50%)
  matrix products  313 us (39%)
  other arithmetic  44.2 us (6%)
  between operations  14.2 us (2%)
  local copies, waits for them, and re-layouts  12.2 us (2%)
    reduce_scatter x1, waiting for transfers between devices, local(): lax.psum_scatter(partial_proj.astype(jnp.bfloat16), 'col', scatter_dimens...  138 us
    dot_general x1, matrix products, block_parts(): scores = jnp.einsum('tjn,sjn->jts', c_block, b_block, precision=highest)  86.9 us
    all_gather x1, waiting for transfers between devices, local(): lax.all_gather(hidden, 'row', axis=0, tiled=True)  83.9 us
    reduce_scatter x1, waiting for transfers between devices, local(): lax.psum_scatter(jnp.dot(all_tokens, w_output, preferred_element_type=jnp...  76.9 us
    dot_general x1, matrix products, local(): jnp.dot(lax.all_gather(hidden, 'row', axis=0, tiled=True), weights, prefe...  74.9 us
    all_gather x1, waiting for transfers between devices, local(): all_tokens = lax.all_gather(y_normed, 'col', axis=0, tiled=True)  57.6 us
    all_gather x1, waiting for transfers between devices, local(): gathered_bc = lax.all_gather(conv_bc, 'row', axis=1, tiled=True)  37.6 us
    dot_general x1, matrix products, local(): jnp.einsum('tjn,jpn->tjp', c_heads, incoming, precision=highest)  34.2 us
  transfers between devices with their start and end apart: 7, of which 5 were waited for; matrix products, arithmetic and copies ran while one was open for 17% of the time, Pallas kernels for 0%

commit v1 on v0

--- a/solution.py
+++ b/solution.py
@@ -1,6 +1,8 @@
 import jax
 import jax.numpy as jnp
 from jax import lax
+from jax.experimental import pallas as pl
+from jax.experimental.pallas import tpu as pltpu
 from jax.sharding import PartitionSpec as P
 
 highest = lax.Precision.HIGHEST
@@ -103,7 +105,7 @@
     return (earlier[0] * later_part[0], later_part[0][:, None, None] * earlier[1] + later_part[1])
 
 
-def local(
+def general(
     hidden,
     w_gate_z,
     w_input_x,
@@ -209,6 +211,212 @@
     )
 
 
+def scan_kernel(x_ref, b_ref, c_ref, dt_ref, cum_ref, dt_t_ref, cum_t_ref, skip_ref, first_ref, y_ref, state):
+    heads = dt_ref.shape[1]
+    size = x_ref.shape[1] // heads
+    length = x_ref.shape[0]
+
+    @pl.when(pl.program_id(0) == 0)
+    def _():
+        state[...] = first_ref[...]
+
+    b = b_ref[...]
+    c = c_ref[...]
+    contract_last = (((1,), (1,)), ((), ()))
+    scores = lax.dot_general(c, b, contract_last, preferred_element_type=jnp.float32)
+    rows = lax.broadcasted_iota(jnp.int32, (length, length), 0)
+    cols = lax.broadcasted_iota(jnp.int32, (length, length), 1)
+    causal = rows >= cols
+    scores = jnp.where(causal, scores, 0.0)
+    carried = lax.dot_general(
+        c, state[...].astype(jnp.bfloat16), contract_last, preferred_element_type=jnp.float32
+    )
+    outs = []
+    weighted = []
+    for h in range(heads):
+        at = slice(h * size, (h + 1) * size)
+        x = x_ref[:, at]
+        xf = x.astype(jnp.float32)
+        cum = cum_ref[:, h : h + 1]
+        cum_t = cum_t_ref[h : h + 1, :]
+        last = cum_t[:, length - 1 : length]
+        mixing = scores * jnp.exp(jnp.minimum(cum - cum_t, 0.0)) * dt_t_ref[h : h + 1, :]
+        intra = jnp.dot(mixing.astype(jnp.bfloat16), x, preferred_element_type=jnp.float32)
+        outs.append(
+            intra + jnp.exp(cum) * carried[:, at] + skip_ref[h : h + 1, 0:1] * xf
+        )
+        weighted.append((xf * (jnp.exp(last - cum) * dt_ref[:, h : h + 1])).astype(jnp.bfloat16))
+    for h in range(0, heads, 2):
+        y_ref[:, h * size : (h + 2) * size] = jnp.concatenate(outs[h : h + 2], axis=1)
+    added = lax.dot_general(
+        jnp.concatenate(weighted, axis=1),
+        b,
+        (((0,), (0,)), ((), ())),
+        preferred_element_type=jnp.float32,
+    )
+    for h in range(heads):
+        at = slice(h * size, (h + 1) * size)
+        decay = jnp.exp(cum_t_ref[h : h + 1, length - 1 : length])
+        state[at, :] = decay * state[at, :] + added[at, :]
+
+
+def scan_heads(x, b, c, dt_t, cum_t, skip, first, block):
+    tokens, width = x.shape
+    heads, n = dt_t.shape[0], b.shape[1]
+    by_rows = lambda w: pl.BlockSpec((block, w), lambda i: (i, 0))
+    by_cols = pl.BlockSpec((heads, block), lambda i: (0, i))
+    return pl.pallas_call(
+        scan_kernel,
+        grid=(tokens // block,),
+        in_specs=[
+            by_rows(width),
+            by_rows(n),
+            by_rows(n),
+            by_rows(heads),
+            by_rows(heads),
+            by_cols,
+            by_cols,
+            pl.BlockSpec((heads, 128), lambda i: (0, 0)),
+            pl.BlockSpec((width, n), lambda i: (0, 0)),
+        ],
+        out_specs=by_rows(width),
+        out_shape=jax.ShapeDtypeStruct((tokens, width), jnp.float32),
+        scratch_shapes=[pltpu.VMEM((width, n), jnp.float32)],
+        compiler_params=pltpu.CompilerParams(vmem_limit_bytes=40 * 2**20),
+        cost_estimate=pl.CostEstimate(
+            flops=2 * tokens * (block * width + 2 * width * n),
+            bytes_accessed=8 * tokens * width,
+            transcendentals=tokens * block * heads,
+        ),
+    )(x, b, c, dt_t.T, cum_t.T, dt_t, cum_t, jnp.broadcast_to(skip[:, None], (heads, 128)), first)
+
+
+def scatter_channels(partial, dim):
+    mine = lax.axis_index("col")
+    core, chip = mine % 2, mine // 2
+    step = partial.shape[dim] // 4
+
+    def block(array, k, width):
+        return lax.dynamic_slice_in_dim(array, k * width, width, dim)
+
+    give = [block(partial, 2 * k + 1 - core, step) for k in range(2)]
+    keep = [block(partial, 2 * k + core, step) for k in range(2)]
+    got = swapped(jnp.concatenate(give, axis=dim), "col", 0)
+    got = [lax.slice_in_dim(got, k * step, (k + 1) * step, axis=dim) for k in range(2)]
+    pair = [a.astype(jnp.float32) + b.astype(jnp.float32) for a, b in zip(keep, got)]
+    far = jnp.where(chip == 0, pair[1], pair[0]).astype(jnp.bfloat16)
+    near = jnp.where(chip == 0, pair[0], pair[1]).astype(jnp.bfloat16)
+    return near.astype(jnp.float32) + swapped(far, "col", 1).astype(jnp.float32)
+
+
+def by_heads(
+    hidden,
+    w_gate_z,
+    w_input_x,
+    w_input_bc,
+    w_input_dt,
+    conv_kernel_x,
+    conv_kernel_bc,
+    conv_state_x,
+    conv_state_bc,
+    dt_bias,
+    a_log,
+    d_skip,
+    norm_gain,
+    ssm_state,
+    w_output,
+):
+    row, col = lax.axis_index("row"), lax.axis_index("col")
+    cols = lax.axis_size("col")
+    rows = lax.axis_size("row")
+    channels = w_gate_z.shape[1] // cols
+    bc_width = w_input_bc.shape[1] // cols
+    heads = w_input_dt.shape[1] // cols
+    head_size, state_size = ssm_state.shape[1:]
+
+    def share(array, dim):
+        width = array.shape[dim] // cols
+        return lax.dynamic_slice_in_dim(array, col * width, width, dim)
+
+    tokens = lax.all_gather(hidden, "row", axis=0, tiled=True)
+    length = tokens.shape[0]
+
+    def project(weights):
+        return jnp.dot(tokens, weights, preferred_element_type=jnp.float32).astype(jnp.bfloat16)
+
+    part_bc = project(w_input_bc)
+    part_dt = lax.dot_general(
+        w_input_dt, tokens, (((0,), (1,)), ((), ())), preferred_element_type=jnp.float32
+    ).astype(jnp.bfloat16)
+    part_x = project(w_input_x)
+    part_z = project(w_gate_z)
+    input_bc = scatter_channels(part_bc, 1).astype(jnp.bfloat16)
+    dt_raw = scatter_channels(part_dt, 0)
+    input_x = scatter_channels(part_x, 1).astype(jnp.bfloat16)
+    gate_z = scatter_channels(part_z, 1).astype(jnp.bfloat16)
+
+    conv_bc = convolve_silu(share(conv_state_bc, 1), input_bc, share(conv_kernel_bc, 1))
+    routes = []
+    for r in range(rows):
+        for c in range(cols):
+            group = (r * cols + c) // 2
+            source = group + (c % 2) * (rows * cols // 2)
+            routes.append((source, r * cols + c))
+    own = lax.ppermute(conv_bc, ("row", "col"), routes)
+    other = swapped(own, "col", 0)
+    even = col % 2 == 0
+    b = jnp.where(even, own, other)
+    c = jnp.where(even, other, own)
+
+    block = 256
+    steps_dt = jax.nn.softplus(dt_raw + share(dt_bias, 0)[:, None])
+    log_decay = steps_dt * (-jnp.exp(share(a_log, 0)))[:, None]
+    upper = (jnp.arange(block)[:, None] <= jnp.arange(block)[None, :]).astype(jnp.float32)
+    cum = jnp.einsum(
+        "hks,st->hkt", log_decay.reshape(heads, length // block, block), upper, precision=highest
+    ).reshape(heads, length)
+    conv_x = convolve_silu(share(conv_state_x, 1), input_x, share(conv_kernel_x, 1))
+    first = share(ssm_state, 0).reshape(heads * head_size, state_size)
+    y = scan_heads(conv_x, b, c, steps_dt, cum, share(d_skip, 0), first, block)
+
+    gated = y * jax.nn.silu(gate_z.astype(jnp.float32))
+    squares = jnp.sum(gated * gated, axis=1)
+    squares = squares + swapped(squares, "col", 0)
+    scale = lax.rsqrt(squares / (2 * channels) + 1e-05)
+    normed = (gated * scale[:, None] * share(norm_gain, 0)[None, :]).astype(jnp.bfloat16)
+
+    across = swapped(normed, "col", 1)
+    beside = swapped(normed, "col", 0)
+    corner = swapped(across, "col", 0)
+
+    def rows_of(k):
+        return lax.dynamic_slice_in_dim(w_output, k * channels, channels, 0)
+
+    mixed = jnp.zeros((length, w_output.shape[1]), jnp.float32)
+    for piece, mask in ((normed, 0), (beside, 1), (across, 2), (corner, 3)):
+        mixed = mixed + jnp.dot(piece, rows_of(col ^ mask), preferred_element_type=jnp.float32)
+    return lax.psum_scatter(
+        mixed.astype(jnp.bfloat16), "row", scatter_dimension=0, tiled=True
+    )
+
+
+def local(*arrays):
+    w_gate_z, w_input_bc, w_input_dt, ssm_state = arrays[1], arrays[3], arrays[4], arrays[13]
+    rows, cols = lax.axis_size("row"), lax.axis_size("col")
+    tokens = arrays[0].shape[0] * rows
+    state_size = ssm_state.shape[2]
+    groups = w_input_bc.shape[1] * rows // (2 * state_size)
+    fits = (
+        cols == 4
+        and w_input_bc.shape[1] == cols * state_size
+        and groups * 2 == rows * cols
+        and w_input_dt.shape[1] % (2 * cols) == 0
+        and w_gate_z.shape[1] % (cols * 128) == 0
+        and tokens % 256 == 0
+    )
+    return by_heads(*arrays) if fits else general(*arrays)
+
+
 def solution(mesh):
     return jax.shard_map(
         local,

time: 793 us -> 484 us (0.61)
  matrix products: 313 us -> 93.8 us
  waiting for transfers between devices: 395 us -> 236 us
  starting transfers between devices: 2.19 us -> 62.3 us
  Pallas kernels: 0 us -> 19.8 us
    dot_general x9, matrix products: 313 us -> 93.8 us  [the longest x3 48.5 us: project(): jnp.dot(tokens, weights, preferred_element_type=jnp.float32)]
    reduce_scatter x2 -> x1, waiting for transfers between devices: 215 us -> 75 us  [by_heads(): lax.psum_scatter(mixed.astype(jnp.bfloat16), 'row', scatter_dimension=0,...]
    all_gather x4 -> x1, waiting for transfers between devices: 179 us -> 85.1 us  [by_heads(): tokens = lax.all_gather(hidden, 'row', axis=0, tiled=True)]
    ppermute x1 -> x14, waiting for transfers between devices: 0.01 us -> 75.5 us  [the longest x13 75.5 us: swapped(): return lax.ppermute(value, axis, pairs)]
    ppermute x1 -> x14, starting transfers between devices: 1.72 us -> 62.3 us  [the longest x13 61.6 us: swapped(): return lax.ppermute(value, axis, pairs)]
    select_n x11 -> x1, other arithmetic: 22.6 us -> 1.27 us  [by_heads(): c = jnp.where(even, other, own)]
    convert_element_type x2 -> x7, other arithmetic: 2.17 us -> 22.4 us  [the longest x4 13.5 us: scatter_channels(): far = jnp.where(chip == 0, pair[1], pair[0]).astype(jnp.bfloat16)]
    pallas_call x0 -> x1, Pallas kernels: none -> 19.8 us  [scan_heads(): pl.pallas_call(scan_kernel, grid=(tokens // block,), in_specs=[by_rows(wi...]
  transfers between devices with their start and end apart: 7 -> 16, of which waited for: 5 -> 7; matrix products, arithmetic and copies ran while one was open for 17% -> 23% of each run, Pallas kernels for 0% -> 4%
where the time goes in v1:
time: 484 us; the launch traced here: 476 us
  waiting for transfers between devices  236 us (49%)
  matrix products  93.8 us (19%)
  starting transfers between devices  62.3 us (13%)
  other arithmetic  38.5 us (8%)
  Pallas kernels  19.8 us (4%)
  between operations  14.2 us (3%)
  local copies, waits for them, and re-layouts  11.4 us (2%)
    all_gather x1, waiting for transfers between devices, by_heads(): tokens = lax.all_gather(hidden, 'row', axis=0, tiled=True)  85.1 us
    ppermute x13, waiting for transfers between devices, swapped(): return lax.ppermute(value, axis, pairs)  75.5 us
    reduce_scatter x1, waiting for transfers between devices, by_heads(): lax.psum_scatter(mixed.astype(jnp.bfloat16), 'row', scatter_dimension=0,...  75 us
    ppermute x13, starting transfers between devices, swapped(): return lax.ppermute(value, axis, pairs)  61.6 us
    dot_general x3, matrix products, project(): jnp.dot(tokens, weights, preferred_element_type=jnp.float32)  48.5 us
    dot_general x4, matrix products, by_heads(): jnp.dot(piece, rows_of(col ^ mask), preferred_element_type=jnp.float32)  43.7 us
    pallas_call x1, Pallas kernels, scan_heads(): pl.pallas_call(scan_kernel, grid=(tokens // block,), in_specs=[by_rows(wi...  19.8 us
    convert_element_type x4, other arithmetic, scatter_channels(): far = jnp.where(chip == 0, pair[1], pair[0]).astype(jnp.bfloat16)  13.5 us
  transfers between devices with their start and end apart: 16, of which 7 were waited for; matrix products, arithmetic and copies ran while one was open for 23% of the time, Pallas kernels for 4%

profile of v1, /device:TPU:0, one launch (start us, length us, event | category | flops | bytes accessed | tf_op | source)
XLA Modules:
  0.0 476.5 jit_solution(2677962699517814790)
XLA Ops:
  7.3 85.1 %all-gather.2.cloned.1.call-done = bf16[1024,2048]{1,0:T(8,128)(2,1)} async-done(((bf16[256,2048]{1,0:T(8,128)(2,1)}), bf16[1024,2048]{1,0:T(8,128)(2,1)}) %all-gather.2.cloned.1.call-update) | async-done | bytes 4194320 | tf_op jit(solution)/shard_map/all_gather | solution.py:341
  92.4 7.9 %convolution_convert_fusion.2 = bf16[1024,1024]{1,0:T(8,128)(2,1)S(1)} fusion(bf16[1024,2048]{1,0:T(8,128)(2,1)} %all-gather.2.cloned.1.call-done, bf16[2048,1024]{1,0:T(8,128)(2,1)} %param.18), kind=kOutput, calls=%fused_computation.40 | convolution fusion | flops 4296015872 | bytes 10485760 | tf_op jit(solution)/shard_map/dot_general | solution.py:345
  102.9 20.2 %convolution_convert_fusion.1 = bf16[1024,4096]{1,0:T(8,128)(2,1)S(1)} fusion(bf16[1024,2048]{1,0:T(8,128)(2,1)S(1)} %copy-done.3, bf16[2048,4096]{1,0:T(8,128)(2,1)} %param.17), kind=kOutput, calls=%fused_computation.2 | convolution fusion | flops 17184063488 | bytes 29360128 | tf_op jit(solution)/shard_map/dot_general | solution.py:345
  123.8 2.6 copy-done.1
  126.4 2.5 pad_maximum_fusion
  128.9 20.4 %convolution_convert_fusion = bf16[1024,4096]{1,0:T(8,128)(2,1)S(1)} fusion(bf16[1024,2048]{1,0:T(8,128)(2,1)S(1)} %copy-done.3, bf16[2048,4096]{1,0:T(8,128)(2,1)} %param.16), kind=kOutput, calls=%fused_computation.1 | convolution fusion | flops 17184063488 | bytes 29360128 | tf_op jit(solution)/shard_map/dot_general | solution.py:345
  150.0 2.6 copy-done.2
  152.6 2.4 pad_maximum_fusion.1
  160.5 10.4 %collective-permute-done.3 = bf16[1024,256]{1,0:T(8,128)(2,1)} collective-permute-done((bf16[1024,256]{1,0:T(8,128)(2,1)}, bf16[1024,256]{1,0:T(8,128)(2,1)}, u32[]{:S(2)}, u32[]{:S(2)}) %collective-permute-start.3) | collective-permute-done | bytes 524320 | tf_op jit(solution)/shard_map/ppermute | solution.py:43
  172.8 6.8 %select_convert_fusion.2 = bf16[1024,1024]{1,0:T(8,128)(2,1)} fusion(pred[]{:T(512)S(6)} %eq.10, bf16[1024,2048]{1,0:T(8,128)(2,1)} %collective-permute-done, bf16[1024,4096]{1,0:T(8,128)(2,1)} %copy-done.1, s32[]{:T(128)S(6)} %select_n.154, s32[]{:T(128)S(6)} %select_n.151), kind=kLoop, calls=%fused_computation.35 | loop fusion | flops 8388608 | bytes 10485769 | tf_op jit(solution)/shard_map/convert_element_type | solution.py:307
  186.7 50.2 %collective-permute-start.5 = (bf16[1024,256]{1,0:T(8,128)(2,1)S(1)}, bf16[1024,256]{1,0:T(8,128)(2,1)}, u32[]{:S(2)}, u32[]{:S(2)}) collective-permute-start(bf16[1024,256]{1,0:T(8,128)(2,1)S(1)} %collective-permute-done.4), channel_id=1, source_target_pairs={{0,1},{1,0},{2,3},{3,2},{4,5},{5,4},{6,7},{7,6},{8,9},{9,8},{10,11... | collective-permute-start | bytes 1572872 | tf_op jit(solution)/shard_map/ppermute | solution.py:43
  236.9 2.4 collective-permute-start.7
  243.5 5.5 %select_convert_fusion = bf16[1024,1024]{1,0:T(8,128)(2,1)S(1)} fusion(pred[]{:T(512)S(6)} %eq.10, bf16[1024,2048]{1,0:T(8,128)(2,1)} %collective-permute-done.8, bf16[1024,4096]{1,0:T(8,128)(2,1)} %copy-done.2, s32[]{:T(128)S(6)} %select_n.154, s32[]{:T(128)S(6)} %select_n.151), kind=kLoop, calls=%fused_computation.29 | loop fusion | flops 8388608 | bytes 10485769 | tf_op jit(solution)/shard_map/convert_element_type | solution.py:307
  250.9 6.6 %add_convert_fusion.2 = bf16[1024,1024]{1,0:T(8,128)(2,1)S(1)} fusion(bf16[1024,1024]{1,0:T(8,128)(2,1)} %collective-permute-done.1, pred[]{:T(512)S(6)} %eq.10, bf16[1024,2048]{1,0:T(8,128)(2,1)} %collective-permute-done, bf16[1024,4096]{1,0:T(8,128)(2,1)} %copy-done.1, s32[]{:T(128)S(6)} %select_n.154, s32[]{:T(128)S(6)} %select_n.151), kind=kLoop, calls=%fused_computation.34 | loop fusion | flops 12582912 | bytes 12582921 | tf_op jit(solution)/shard_map/convert_element_type | solution.py:355
  258.2 2.8 multiply_convert_fusion.1.x_ref
  261.1 19.8 %shard_map.145 = f32[1024,1024]{1,0:T(8,128)S(1)} custom-call(bf16[1024,1024]{1,0:T(8,128)(2,1)S(1)} %multiply_convert_fusion.1.x_ref, bf16[1024,256]{1,0:T(8,128)(2,1)S(1)} %get-tuple-element.16.b_ref, bf16[1024,256]{1,0:T(8,128)(2,1)S(1)} %get-tuple-element.15.c_ref, f32[1024,16]{1,0:T(8,128)S(1)} %copy.18.dt_ref, f32[1024,16]{1,0:T(8,128)S(1)} %copy.19.cum_ref, ...), custom_call_target="tpu_custom_call" | custom-call | flops 1610612736 | bytes 8388608 | tf_op jit(solution)/shard_map/pallas_call | solution.py:268
  281.0 15.6 %collective-permute-done.9 = bf16[1024,1024]{1,0:T(8,128)(2,1)S(1)} collective-permute-done((bf16[1024,1024]{1,0:T(8,128)(2,1)S(1)}, bf16[1024,1024]{1,0:T(8,128)(2,1)S(1)}, u32[]{:S(2)}, u32[]{:S(2)}) %collective-permute-start.9) | collective-permute-done | bytes 2097184 | tf_op jit(solution)/shard_map/ppermute | solution.py:43
  296.5 4.3 multiply_reduce_fusion
  303.9 46.5 %collective-permute-done.12 = bf16[1024,1024]{1,0:T(8,128)(2,1)} collective-permute-done((bf16[1024,1024]{1,0:T(8,128)(2,1)S(1)}, bf16[1024,1024]{1,0:T(8,128)(2,1)}, u32[]{:S(2)}, u32[]{:S(2)}) %collective-permute-start.12) | collective-permute-done | bytes 2097184 | tf_op jit(solution)/shard_map/ppermute | solution.py:43
  350.4 9.1 %fusion.13 = f32[1024,2048]{1,0:T(8,128)} fusion(bf16[1024,1024]{1,0:T(8,128)(2,1)S(1)} %multiply_convert_fusion, bf16[4096,2048]{1,0:T(8,128)(2,1)} %param.29, s32[]{:T(128)} %select_n.147), kind=kOutput, calls=%fused_computation.24 | convolution fusion | flops 4294967296 | bytes 14680576 | tf_op jit(solution)/shard_map/dot_general | solution.py:397
  359.6 10.6 %fusion.9 = f32[1024,2048]{1,0:T(8,128)} fusion(bf16[1024,1024]{1,0:T(8,128)(2,1)} %collective-permute-done.12, bf16[4096,2048]{1,0:T(8,128)(2,1)} %param.29, s32[]{:T(128)S(6)} %select_n.180), kind=kOutput, calls=%fused_computation.20 | convolution fusion | flops 4294967296 | bytes 14680068 | tf_op jit(solution)/shard_map/dot_general | solution.py:397
  370.2 10.6 %fusion.11 = f32[1024,2048]{1,0:T(8,128)} fusion(bf16[1024,1024]{1,0:T(8,128)(2,1)} %collective-permute-done.11, bf16[4096,2048]{1,0:T(8,128)(2,1)} %param.29, s32[]{:T(128)S(6)} %select_n.179), kind=kOutput, calls=%fused_computation.22 | convolution fusion | flops 4294967296 | bytes 14680068 | tf_op jit(solution)/shard_map/dot_general | solution.py:397
  380.8 13.3 %add_convert_fusion = bf16[1024,2048]{1,0:T(8,128)(2,1)} fusion(f32[1024,2048]{1,0:T(8,128)} %fusion.9, f32[1024,2048]{1,0:T(8,128)} %fusion.13, f32[1024,2048]{1,0:T(8,128)} %fusion.11, bf16[1024,1024]{1,0:T(8,128)(2,1)S(1)} %collective-permute-done.13, bf16[4096,2048]{1,0:T(8,128)(2,1)} %param.29, s32[]{:T(128)S(6)} %select_n.181), kind=kOutput, calls=%fused_computation | convolution fusion | flops 4303355904 | bytes 35651588 | tf_op jit(solution)/shard_map/dot_general | solution.py:397
  394.1 75.0 %reduce-scatter.2.cloned.1.call-done = bf16[256,2048]{1,0:T(8,128)(2,1)} async-done(((bf16[1024,2048]{1,0:T(8,128)(2,1)}), bf16[256,2048]{1,0:T(8,128)(2,1)}) %reduce-scatter.2.cloned.1.call-update) | async-done | bytes 1048592 | tf_op jit(solution)/shard_map/reduce_scatter | solution.py:398
  (86 shorter events, 28.7 us)
Async XLA Ops:
  6.5 176.0 %copy-start = (bf16[2048,64]{0,1:T(8,128)(2,1)S(1)}, bf16[2048,64]{0,1:T(8,128)(2,1)}, u32[]{:S(2)}) copy-start(bf16[2048,64]{0,1:T(8,128)(2,1)} %param.19) | copy-start | bytes 786436
  6.5 85.9 %all-gather.2.cloned.1.call-start = ((), (), s32[]{:S(2)}) async-start(), calls=%async_computation.1 | async-start | bytes 5242880 | tf_op jit(solution)/shard_map/all_gather | solution.py:341
  7.3 461.9 %reduce-scatter.2.cloned.1.call-start = ((), (), s32[]{:S(2)}) async-start(), calls=%async_computation.2 | async-start | bytes 5242880 | tf_op jit(solution)/shard_map/reduce_scatter | solution.py:398
  101.6 53.9 %collective-permute-start.2 = (bf16[1024,512]{1,0:T(8,128)(2,1)}, bf16[1024,512]{1,0:T(8,128)(2,1)S(1)}, u32[]{:S(2)}, u32[]{:S(2)}) collective-permute-start(bf16[1024,512]{1,0:T(8,128)(2,1)} %pad_maximum_fusion.2), channel_id=1, source_target_pairs={{0,1},{1,0},{2,3},{3,2},{4,5},{5,4},{6,7},{7,6},{8,9},{9,8},{10,11... | collective-permute-start | bytes 3145736 | tf_op jit(solution)/shard_map/ppermute | solution.py:43
  128.9 43.9 %collective-permute-start = (bf16[1024,2048]{1,0:T(8,128)(2,1)}, bf16[1024,2048]{1,0:T(8,128)(2,1)}, u32[]{:S(2)}, u32[]{:S(2)}) collective-permute-start(bf16[1024,2048]{1,0:T(8,128)(2,1)} %pad_maximum_fusion), channel_id=1, source_target_pairs={{0,1},{1,0},{2,3},{3,2},{4,5},{5,4},{6,7},{7,6},{8,9},{9,8},{10,11... | collective-permute-start | bytes 12582920 | tf_op jit(solution)/shard_map/ppermute | solution.py:43
  155.0 88.5 %collective-permute-start.8 = (bf16[1024,2048]{1,0:T(8,128)(2,1)}, bf16[1024,2048]{1,0:T(8,128)(2,1)}, u32[]{:S(2)}, u32[]{:S(2)}) collective-permute-start(bf16[1024,2048]{1,0:T(8,128)(2,1)} %pad_maximum_fusion.1), channel_id=1, source_target_pairs={{0,1},{1,0},{2,3},{3,2},{4,5},{5,4},{6,7},{7,6},{8,9},{9,8},{10,11... | collective-permute-start | bytes 12582920 | tf_op jit(solution)/shard_map/ppermute | solution.py:43
  156.7 14.2 %collective-permute-start.3 = (bf16[1024,256]{1,0:T(8,128)(2,1)}, bf16[1024,256]{1,0:T(8,128)(2,1)}, u32[]{:S(2)}, u32[]{:S(2)}) collective-permute-start(bf16[1024,256]{1,0:T(8,128)(2,1)} %select_convert_fusion.4), channel_id=1, source_target_pairs={{0,2},{1,3},{2,0},{3,1},{4,6},{5,7},{6,4},{7,5},{8,10},{9,11},{10,... | collective-permute-start | bytes 1572872 | tf_op jit(solution)/shard_map/ppermute | solution.py:43
  179.6 71.3 %collective-permute-start.1 = (bf16[1024,1024]{1,0:T(8,128)(2,1)}, bf16[1024,1024]{1,0:T(8,128)(2,1)}, u32[]{:S(2)}, u32[]{:S(2)}) collective-permute-start(bf16[1024,1024]{1,0:T(8,128)(2,1)} %select_convert_fusion.2), channel_id=1, source_target_pairs={{0,2},{1,3},{2,0},{3,1},{4,6},{5,7},{6,4},{7,5},{8,10},{9,11},{10,... | collective-permute-start | bytes 6291464 | tf_op jit(solution)/shard_map/ppermute | solution.py:43
  181.2 58.2 %copy-start.9 = (f32[64]{0:T(128)S(1)}, f32[64]{0:T(128)}, u32[]{:S(2)}) copy-start(f32[64]{0:T(128)} %param.25) | copy-start | bytes 772
  181.2 58.3 %copy-start.10 = (f32[64]{0:T(128)S(1)}, f32[64]{0:T(128)}, u32[]{:S(2)}) copy-start(f32[64]{0:T(128)} %param.24) | copy-start | bytes 772
  181.2 58.4 %copy-start.11 = (f32[64]{0:T(128)S(1)}, f32[64]{0:T(128)}, u32[]{:S(2)}) copy-start(f32[64]{0:T(128)} %param.26) | copy-start | bytes 772
  181.8 4.9 %collective-permute-start.4 = (bf16[1024,256]{1,0:T(8,128)(2,1)S(1)}, bf16[1024,256]{1,0:T(8,128)(2,1)S(1)}, u32[]{:S(2)}, u32[]{:S(2)}) collective-permute-start(bf16[1024,256]{1,0:T(8,128)(2,1)S(1)} %multiply_convert_fusion.2), channel_id=1, source_target_pairs={{0,0},{8,1},{1,2},{9,3},{2,4},{10,5},{3,6},{11,7},{4,8},{12,9},{5,... | collective-permute-start | bytes 1572872 | tf_op jit(solution)/shard_map/ppermute | solution.py:365
  184.0 53.0 %collective-permute-start.6 = (bf16[32,1024]{1,0:T(8,128)(2,1)S(1)}, bf16[32,1024]{1,0:T(8,128)(2,1)S(1)}, u32[]{:S(2)}, u32[]{:S(2)}) collective-permute-start(bf16[32,1024]{1,0:T(8,128)(2,1)S(1)} %pad_maximum_fusion.3), channel_id=1, source_target_pairs={{0,1},{1,0},{2,3},{3,2},{4,5},{5,4},{6,7},{7,6},{8,9},{9,8},{10,11... | collective-permute-start | bytes 196616 | tf_op jit(solution)/shard_map/ppermute | solution.py:43
  186.7 55.5 %copy-start.6 = (bf16[1024,256]{1,0:T(8,128)(2,1)}, bf16[1024,256]{1,0:T(8,128)(2,1)S(1)}, u32[]{:S(2)}) copy-start(bf16[1024,256]{1,0:T(8,128)(2,1)S(1)} %collective-permute-done.4) | copy-start | bytes 1572868
  186.7 55.5 %collective-permute-start.5 = (bf16[1024,256]{1,0:T(8,128)(2,1)S(1)}, bf16[1024,256]{1,0:T(8,128)(2,1)}, u32[]{:S(2)}, u32[]{:S(2)}) collective-permute-start(bf16[1024,256]{1,0:T(8,128)(2,1)S(1)} %collective-permute-done.4), channel_id=1, source_target_pairs={{0,1},{1,0},{2,3},{3,2},{4,5},{5,4},{6,7},{7,6},{8,9},{9,8},{10,11... | collective-permute-start | bytes 1572872 | tf_op jit(solution)/shard_map/ppermute | solution.py:43
  236.9 4.5 collective-permute-start.7
  249.0 47.5 %collective-permute-start.9 = (bf16[1024,1024]{1,0:T(8,128)(2,1)S(1)}, bf16[1024,1024]{1,0:T(8,128)(2,1)S(1)}, u32[]{:S(2)}, u32[]{:S(2)}) collective-permute-start(bf16[1024,1024]{1,0:T(8,128)(2,1)S(1)} %select_convert_fusion), channel_id=1, source_target_pairs={{0,2},{1,3},{2,0},{3,1},{4,6},{5,7},{6,4},{7,5},{8,10},{9,11},{10,... | collective-permute-start | bytes 6291464 | tf_op jit(solution)/shard_map/ppermute | solution.py:43
  257.6 38.9 %slice-start = ((s8[8388608]{0:T(1024)(128)(4,1)}), s8[4194304]{0:T(1024)(128)(4,1)S(1)}, s32[]{:S(2)}) async-start(s8[8388608]{0:T(1024)(128)(4,1)} %bitcast.38), calls=%async_computation.3 | async-start | bytes 8388608
  258.2 38.3 %slice-start.1 = ((s8[8388608]{0:T(1024)(128)(4,1)}), s8[4194304]{0:T(1024)(128)(4,1)S(1)}, s32[]{:S(2)}) async-start(s8[8388608]{0:T(1024)(128)(4,1)} %bitcast.38), calls=%async_computation.4 | async-start | bytes 8388608
  280.9 21.2 %dynamic-slice-start = ((f32[4096]{0:T(1024)}, s32[]{:T(128)}), f32[1024]{0:T(1024)S(1)}, s32[]{:S(2)}) async-start(f32[4096]{0:T(1024)} %param.27, s32[]{:T(128)} %select_n.147), calls=%async_computation.5 | async-start | bytes 8704 | tf_op jit(solution)/shard_map/dynamic_slice | solution.py:339
  300.9 1.2 collective-permute-start.10
  302.6 47.9 %collective-permute-start.12 = (bf16[1024,1024]{1,0:T(8,128)(2,1)S(1)}, bf16[1024,1024]{1,0:T(8,128)(2,1)}, u32[]{:S(2)}, u32[]{:S(2)}) collective-permute-start(bf16[1024,1024]{1,0:T(8,128)(2,1)S(1)} %multiply_convert_fusion), channel_id=1, source_target_pairs={{0,2},{1,3},{2,0},{3,1},{4,6},{5,7},{6,4},{7,5},{8,10},{9,11},{10,... | collective-permute-start | bytes 6291464 | tf_op jit(solution)/shard_map/ppermute | solution.py:43
  303.9 66.2 %collective-permute-start.11 = (bf16[1024,1024]{1,0:T(8,128)(2,1)S(1)}, bf16[1024,1024]{1,0:T(8,128)(2,1)}, u32[]{:S(2)}, u32[]{:S(2)}) collective-permute-start(bf16[1024,1024]{1,0:T(8,128)(2,1)S(1)} %multiply_convert_fusion), channel_id=1, source_target_pairs={{0,1},{1,0},{2,3},{3,2},{4,5},{5,4},{6,7},{7,6},{8,9},{9,8},{10,11... | collective-permute-start | bytes 6291464 | tf_op jit(solution)/shard_map/ppermute | solution.py:43
  350.4 30.3 %collective-permute-start.13 = (bf16[1024,1024]{1,0:T(8,128)(2,1)}, bf16[1024,1024]{1,0:T(8,128)(2,1)S(1)}, u32[]{:S(2)}, u32[]{:S(2)}) collective-permute-start(bf16[1024,1024]{1,0:T(8,128)(2,1)} %collective-permute-done.12), channel_id=1, source_target_pairs={{0,1},{1,0},{2,3},{3,2},{4,5},{5,4},{6,7},{7,6},{8,9},{9,8},{10,11... | collective-permute-start | bytes 6291464 | tf_op jit(solution)/shard_map/ppermute | solution.py:43
  (7 other events, 28.3 us)
Sparse Core Ops, SparseCore 0:
  8.9 83.4 all-gather.1
  394.3 74.8 reduce-scatter.1
